TPU v7x, 512 devices: a whole 4x8x8 slice. The times are simulated.
512 devices in a mesh: label: 64 (over y, x, core), query: 8 (over z).
Axes of the slice: x: 4, y: 8, z: 8, core: 2. Of those that a mesh axis runs over, the one named last changes fastest.
Arguments:
- queries: bfloat16 [1536, 768], P('query'), may hold values from -6 to 6
- label_ids: int32 [1536, 10], P('query'), may hold values from 0 to 4095, as said below
- label_text: bfloat16 [4096, 32, 768], P('label'), may hold values from -16 to 16
- up_weight: bfloat16 [768, 3072], P(None, 'query'), may hold values from -0.21875 to 0.21875
- down_weight: bfloat16 [768, 3072], P(None, 'query'), may hold values from -0.109375 to 0.109375
- free_vectors: float32 [4096, 768], P('label'), may hold values from -4 to 4
- moments: float32 [4096, 768], P('label'), may hold values from -0.06 to 0.06
- seconds: float32 [4096, 768], P('label'), may hold values from 1e-05 to 0.001
Outputs:
- free_new: float32 [4096, 768], P('label')
- moments_new: float32 [4096, 768], P('label')
- seconds_new: float32 [4096, 768], P('label')
- query_grad: float32 [1536, 768], P('query')
- up_grad: float32 [768, 3072], P('label', 'query')
- down_grad: float32 [768, 3072], P('label', 'query')
Inputs may be any that keep to these rules, and one draw needn't show every extreme that they name: `label_ids`: the 10 ids of one query are distinct.
All inputs are finite; a program needn't handle non-finite values.
Results may differ from a plain program's by a relative error of at most 0.023.
Values sent between devices are 32-bit elements; how exact they have to be, the bound alone decides.
A program may use at most 64 MiB of HBM per device.

v0:
```python
import jax
import jax.numpy as jnp
from jax import lax
from jax.sharding import PartitionSpec as P

beta_one = 0.9
beta_two = 0.999
adam_eps = 1e-08
learn_rate = 0.05
first_fix = 1.0 - 0.9**10
second_fix = 1.0 - 0.999**10


def gelu_tanh(values):
    return jax.nn.gelu(values, approximate=True)


def body(queries, label_ids, label_text, up_weight, down_weight, free_vectors, moments, seconds):
    label_rows, text_len, model_width = label_text.shape
    unit_cols = up_weight.shape[1]
    temper = 1.0 / jnp.sqrt(jnp.float32(model_width))
    text_rows = label_text.reshape(label_rows * text_len, model_width)
    preact = jnp.dot(text_rows, up_weight, preferred_element_type=jnp.float32)
    hidden = gelu_tanh(preact).astype(jnp.bfloat16)
    pooled_hidden = jnp.mean(
        hidden.reshape(label_rows, text_len, unit_cols), axis=1, dtype=jnp.float32
    )
    pooled_text = jnp.mean(label_text, axis=1, dtype=jnp.float32)
    encoded_part = jnp.einsum(
        "lf,df->ld", pooled_hidden, down_weight.astype(jnp.float32), precision=lax.Precision.HIGHEST
    )
    encoded = lax.psum(encoded_part, "query")
    label_vec = pooled_text + encoded + free_vectors
    label_bf = label_vec.astype(jnp.bfloat16)
    first_label = lax.axis_index("label") * label_rows
    local_ids = label_ids - first_label
    owners = (
        local_ids[:, :, None] == jnp.arange(label_rows, dtype=jnp.int32)[None, None, :]
    ).astype(jnp.float32)
    similar = jnp.einsum("id,jd->ij", queries, label_bf, preferred_element_type=jnp.float32)
    partial_value = jnp.einsum("ikj,ij->ik", owners, similar, precision=lax.Precision.HIGHEST)
    scores = lax.psum(partial_value, "label") * temper
    likely = jax.nn.softmax(scores, axis=-1)
    target = jnp.where(jnp.arange(scores.shape[1]) < 2, 0.5, 0.0).astype(jnp.float32)
    pair_coef = ((likely - target[None, :]) * temper).astype(jnp.bfloat16)
    spread = jnp.einsum(
        "ik,ikj->ij", pair_coef.astype(jnp.float32), owners, precision=lax.Precision.HIGHEST
    ).astype(jnp.bfloat16)
    query_terms = jnp.dot(spread, label_bf, preferred_element_type=jnp.float32)
    query_grad = lax.psum(query_terms, "label")
    grad_part = jnp.einsum("ij,id->jd", spread, queries, preferred_element_type=jnp.float32)
    count_part = jnp.sum(owners, axis=(0, 1))
    label_grad, counts = lax.psum((grad_part, count_part), "query")
    out_grad = label_grad.astype(jnp.bfloat16)
    hidden_grad = jnp.dot(out_grad, down_weight, preferred_element_type=jnp.float32) / text_len
    token_grad = jnp.broadcast_to(
        hidden_grad[:, None, :], (label_rows, text_len, unit_cols)
    ).reshape(label_rows * text_len, unit_cols)
    preact_grad = jax.vjp(gelu_tanh, preact)[1](token_grad)[0].astype(jnp.bfloat16)
    joined = lax.psum_scatter(
        jnp.concatenate(
            (
                lax.dot_general(
                    text_rows,
                    preact_grad,
                    (((0,), (0,)), ((), ())),
                    preferred_element_type=jnp.float32,
                ),
                jnp.einsum(
                    "ld,lf->df",
                    out_grad.astype(jnp.float32),
                    pooled_hidden,
                    precision=lax.Precision.HIGHEST,
                ),
            ),
            axis=1,
        ),
        "label",
        scatter_dimension=0,
        tiled=True,
    )
    up_part = joined[:, :unit_cols]
    down_part = joined[:, unit_cols:]
    touched = (counts > 0.5)[:, None]
    moment_step = beta_one * moments + (1.0 - beta_one) * label_grad
    second_step = beta_two * seconds + (1.0 - beta_two) * label_grad * label_grad
    update = (
        learn_rate * (moment_step / first_fix) / (jnp.sqrt(second_step / second_fix) + adam_eps)
    )
    free_new = jnp.where(touched, free_vectors - update, free_vectors)
    moments_new = jnp.where(touched, moment_step, moments)
    seconds_new = jnp.where(touched, second_step, seconds)
    return (free_new, moments_new, seconds_new, query_grad, up_part, down_part)


def solution(mesh):
    placed = (
        P("query", None),
        P("query", None),
        P("label", None, None),
        P(None, "query"),
        P(None, "query"),
        P("label", None),
        P("label", None),
        P("label", None),
    )
    return jax.shard_map(
        body,
        mesh=mesh,
        in_specs=placed,
        out_specs=(
            P("label", None),
            P("label", None),
            P("label", None),
            P("query", None),
            P("label", "query"),
            P("label", "query"),
        ),
        check_vma=False,
    )
```

profile of v0, /device:TPU:25, one launch (start us, length us, event | category | flops | bytes accessed | tf_op | source)
XLA Modules:
  0.0 643.8 jit_solution(12416014666471665310)
XLA Ops:
  7.2 1.0 copy-done
  8.2 6.1 convert_reduce_fusion.1
  14.4 1.3 fusion.16
  15.8 2.9 convert_reduce_fusion
  18.7 75.3 %all-reduce.6.cloned.1.call-done = f32[64,768]{1,0:T(8,128)} async-done(((f32[64,768]{1,0:T(8,128)}), f32[64,768]{1,0:T(8,128)}) %all-reduce.6.cloned.1.call-update) | async-done | bytes 196624 | tf_op jit(solution)/shard_map/psum | solution.py:32
  94.0 1.0 add_convert_fusion
  95.3 235.5 %psum.37 = f32[192,10]{0,1:T(8,128)S(1)} all-reduce(f32[192,10]{0,1:T(8,128)S(1)} %select_reduce_fusion.1), channel_id=1, replica_groups=mesh['label'=64,'query'=8] {'label'}, use_global_device_ids=true, to_apply=%region_5.0 | all-reduce | flops 1920 | bytes 15360 | tf_op jit(solution)/shard_map/psum | solution.py:42
  330.9 0.2 convert_reduce_fusion.2
  331.3 0.9 fusion.32
  332.3 1.0 fusion.31
  333.3 83.8 %all-reduce.8.cloned.1.call-done = f32[64,768]{1,0:T(8,128)} async-done(((f32[64,768]{1,0:T(8,128)}), f32[64,768]{1,0:T(8,128)}) %all-reduce.8.cloned.1.call-update) | async-done | bytes 196624 | tf_op jit(solution)/shard_map/psum | solution.py:53
  417.1 1.3 convolution_multiply_fusion
  418.4 3.6 fusion.6
  422.0 1.4 convolution_bitcast_fusion
  423.5 0.7 fusion.14
  424.2 1.5 pad_maximum_fusion
  425.7 1.3 dynamic-slice
  427.7 12.6 %psum.35 = f32[64]{0:T(128)S(1)} all-reduce(f32[64]{0:T(128)S(1)} %get-tuple-element.24), channel_id=1, replica_groups=mesh['label'=64,'query'=8] {'query'}, use_global_device_ids=true, to_apply=%region_1.0 | all-reduce | flops 64 | bytes 512 | tf_op jit(solution)/shard_map/psum | solution.py:53
  440.3 1.0 fusion.13
  441.3 191.3 %all-reduce.10.cloned.1.call-done = (f32[192,768]{1,0:T(8,128)}, f32[768,768]{0,1:T(8,128)}) async-done(((f32[192,768]{1,0:T(8,128)}, f32[768,768]{0,1:T(8,128)}), (f32[192,768]{1,0:T(8,128)}, f32[768,768]{0,1:T(8,128)})) %all-reduce.10.cloned.1.call-update) | async-done | bytes 2949136 | tf_op jit(solution)/shard_map/psum | solution.py:50
  632.7 1.3 fusion.30
  633.9 0.7 copy.20
  634.7 0.7 copy.21
  635.4 1.9 copy.41
  (32 shorter events, 0.8 us)
Async XLA Ops:
  7.2 1.1 copy-start
  7.2 86.8 %all-reduce.6.cloned.1.call-start = ((), (), s32[]{:S(2)}) async-start(), calls=%async_computation | async-start | bytes 393216 | tf_op jit(solution)/shard_map/psum | solution.py:32
  8.2 6.1 copy-start.2
  14.4 4.3 copy-start.8
  14.4 79.7 %copy-start.5 = (f32[64,768]{1,0:T(8,128)S(1)}, f32[64,768]{1,0:T(8,128)}, u32[]{:S(2)}) copy-start(f32[64,768]{1,0:T(8,128)} %param.13) | copy-start | bytes 589828
  14.4 80.6 %copy-start.4 = (bf16[192,768]{1,0:T(8,128)(2,1)S(1)}, bf16[192,768]{1,0:T(8,128)(2,1)}, u32[]{:S(2)}) copy-start(bf16[192,768]{1,0:T(8,128)(2,1)} %param.8) | copy-start | bytes 884740
  15.7 401.4 %all-reduce.8.cloned.1.call-start = ((), (), s32[]{:S(2)}) async-start(), calls=%async_computation.1 | async-start | bytes 393216 | tf_op jit(solution)/shard_map/psum | solution.py:53
  332.2 300.4 %all-reduce.10.cloned.1.call-start = ((), (), s32[]{:S(2)}) async-start(), calls=%async_computation.2 | async-start | bytes 5898240 | tf_op jit(solution)/shard_map/psum | solution.py:50
  417.1 4.9 copy-start.1
  422.0 1.5 copy-start.3
  424.2 16.2 %copy-start.6 = (f32[64,768]{1,0:T(8,128)S(1)}, f32[64,768]{1,0:T(8,128)}, u32[]{:S(2)}) copy-start(f32[64,768]{1,0:T(8,128)} %param.15) | copy-start | bytes 589828
  424.2 16.2 %copy-start.7 = (f32[64,768]{1,0:T(8,128)S(1)}, f32[64,768]{1,0:T(8,128)}, u32[]{:S(2)}) copy-start(f32[64,768]{1,0:T(8,128)} %param.14) | copy-start | bytes 589828
Sparse Core Ops, SparseCore 0:
  15.8 78.1 all-reduce.5
  332.3 84.7 all-reduce.7
  425.9 206.7 all-reduce.9
where the time goes:
time: 644 us
  waiting for transfers between devices  351 us (55%)
  blocking collectives  248 us (39%)
  between operations  14.6 us (2%)
  matrix products  13 us (2%)
  other arithmetic  10.4 us (2%)
  local copies, waits for them, and re-layouts  7.07 us (1%)
    psum x1, blocking collectives, body(): scores = lax.psum(partial_value, 'label') * temper  235 us
    psum x1, waiting for transfers between devices, body(): query_grad = lax.psum(query_terms, 'label')  191 us
    psum x1, waiting for transfers between devices, body(): label_grad, counts = lax.psum((grad_part, count_part), 'query')  83.8 us
    psum x1, waiting for transfers between devices, body(): encoded = lax.psum(encoded_part, 'query')  75.3 us
  transfers between devices with their start and end apart: 3, of which 3 were waited for; matrix products, arithmetic and copies ran while one was open for 1% of the time, Pallas kernels for 0%

commit v1 on v0

--- a/solution.py
+++ b/solution.py
@@ -39,7 +39,7 @@
     ).astype(jnp.float32)
     similar = jnp.einsum("id,jd->ij", queries, label_bf, preferred_element_type=jnp.float32)
     partial_value = jnp.einsum("ikj,ij->ik", owners, similar, precision=lax.Precision.HIGHEST)
-    scores = lax.psum(partial_value, "label") * temper
+    scores = jnp.sum(lax.all_gather(partial_value, "label"), axis=0) * temper
     likely = jax.nn.softmax(scores, axis=-1)
     target = jnp.where(jnp.arange(scores.shape[1]) < 2, 0.5, 0.0).astype(jnp.float32)
     pair_coef = ((likely - target[None, :]) * temper).astype(jnp.bfloat16)

time: 644 us -> 449 us (0.70)
  blocking collectives: 248 us -> 67.9 us
  waiting for transfers between devices: 351 us -> 335 us
    psum x1 -> x0, blocking collectives: 235 us -> none  [body(): scores = lax.psum(partial_value, 'label') * temper]
    all_gather x0 -> x1, blocking collectives: none -> 55.3 us  [body(): scores = jnp.sum(lax.all_gather(partial_value, 'label'), axis=0) * temper]
    psum x1, waiting for transfers between devices: 83.8 us -> 68.7 us  [body(): label_grad, counts = lax.psum((grad_part, count_part), 'query')]
where the time goes in v1:
time: 449 us; the launch traced here: 448 us
  waiting for transfers between devices  335 us (75%)
  blocking collectives  67.9 us (15%)
  between operations  14.6 us (3%)
  matrix products  13 us (3%)
  other arithmetic  10.5 us (2%)
  local copies, waits for them, and re-layouts  7.07 us (2%)
    psum x1, waiting for transfers between devices, body(): query_grad = lax.psum(query_terms, 'label')  191 us
    psum x1, waiting for transfers between devices, body(): encoded = lax.psum(encoded_part, 'query')  75.3 us
    psum x1, waiting for transfers between devices, body(): label_grad, counts = lax.psum((grad_part, count_part), 'query')  68.7 us
    all_gather x1, blocking collectives, body(): scores = jnp.sum(lax.all_gather(partial_value, 'label'), axis=0) * temper  55.3 us
    psum x1, blocking collectives, body(): label_grad, counts = lax.psum((grad_part, count_part), 'query')  12.6 us
  transfers between devices with their start and end apart: 3, of which 3 were waited for; matrix products, arithmetic and copies ran while one was open for 1% of the time, Pallas kernels for 0%

profile of v1, /device:TPU:25, one launch (start us, length us, event | category | flops | bytes accessed | tf_op | source)
XLA Modules:
  0.0 448.2 jit_solution(595944350902048428)
XLA Ops:
  7.2 1.0 copy-done
  8.2 6.1 %convert_reduce_fusion.1 = (f32[64,384]{1,0:T(8,128)S(1)}, f32[2048,384]{1,0:T(8,128)}) fusion(bf16[2048,768]{1,0:T(8,128)(2,1)} %bitcast.41, bf16[768,384]{1,0:T(8,128)(2,1)S(1)} %copy-done), kind=kOutput, calls=%fused_computation.15 | convolution fusion | flops 1216585728 | bytes 6979584 | tf_op jit(solution)/shard_map/dot_general | solution.py:23
  14.4 1.3 fusion.16
  15.8 2.9 convert_reduce_fusion
  18.7 75.3 %all-reduce.6.cloned.1.call-done = f32[64,768]{1,0:T(8,128)} async-done(((f32[64,768]{1,0:T(8,128)}), f32[64,768]{1,0:T(8,128)}) %all-reduce.6.cloned.1.call-update) | async-done | bytes 196624 | tf_op jit(solution)/shard_map/psum | solution.py:32
  94.0 1.0 add_convert_fusion
  95.3 55.3 %all-gather.1 = f32[64,192,10]{1,2,0:T(8,128)S(1)} all-gather(f32[1,192,10]{1,2,0:T(8,128)S(1)} %bitcast.43), channel_id=2, replica_groups=mesh['label'=64,'query'=8] {'label'}, dimensions={0}, use_global_device_ids=true | all-gather | bytes 499200 | tf_op jit(solution)/shard_map/all_gather | solution.py:42
  150.8 0.2 convert_reduce_fusion.2
  151.2 0.9 fusion.32
  152.1 1.0 fusion.31
  153.2 68.7 %all-reduce.8.cloned.1.call-done = f32[64,768]{1,0:T(8,128)} async-done(((f32[64,768]{1,0:T(8,128)}), f32[64,768]{1,0:T(8,128)}) %all-reduce.8.cloned.1.call-update) | async-done | bytes 196624 | tf_op jit(solution)/shard_map/psum | solution.py:53
  221.8 1.3 convolution_multiply_fusion
  223.1 3.6 fusion.6
  226.7 1.4 convolution_bitcast_fusion
  228.2 0.7 fusion.14
  228.9 1.5 pad_maximum_fusion
  230.5 1.3 dynamic-slice
  232.4 12.6 %psum.28 = f32[64]{0:T(128)S(1)} all-reduce(f32[64]{0:T(128)S(1)} %get-tuple-element.30), channel_id=1, replica_groups=mesh['label'=64,'query'=8] {'query'}, use_global_device_ids=true, to_apply=%region_1.0 | all-reduce | flops 64 | bytes 512 | tf_op jit(solution)/shard_map/psum | solution.py:53
  245.0 1.0 fusion.13
  246.0 191.0 %all-reduce.10.cloned.1.call-done = (f32[192,768]{1,0:T(8,128)}, f32[768,768]{0,1:T(8,128)}) async-done(((f32[192,768]{1,0:T(8,128)}, f32[768,768]{0,1:T(8,128)}), (f32[192,768]{1,0:T(8,128)}, f32[768,768]{0,1:T(8,128)})) %all-reduce.10.cloned.1.call-update) | async-done | bytes 2949136 | tf_op jit(solution)/shard_map/psum | solution.py:50
  437.0 1.3 fusion.30
  438.3 0.7 copy.23
  439.0 0.7 copy.24
  439.7 1.9 copy.44
  (33 shorter events, 0.9 us)
Async XLA Ops:
  7.2 1.1 copy-start
  7.2 86.8 %all-reduce.6.cloned.1.call-start = ((), (), s32[]{:S(2)}) async-start(), calls=%async_computation | async-start | bytes 393216 | tf_op jit(solution)/shard_map/psum | solution.py:32
  8.2 6.1 %copy-start.2 = (bf16[768,384]{1,0:T(8,128)(2,1)S(1)}, bf16[768,384]{1,0:T(8,128)(2,1)}, u32[]{:S(2)}) copy-start(bf16[768,384]{1,0:T(8,128)(2,1)} %param.12) | copy-start | bytes 1769476
  14.4 4.3 copy-start.8
  14.4 79.7 %copy-start.5 = (f32[64,768]{1,0:T(8,128)S(1)}, f32[64,768]{1,0:T(8,128)}, u32[]{:S(2)}) copy-start(f32[64,768]{1,0:T(8,128)} %param.13) | copy-start | bytes 589828
  14.4 80.6 %copy-start.4 = (bf16[192,768]{1,0:T(8,128)(2,1)S(1)}, bf16[192,768]{1,0:T(8,128)(2,1)}, u32[]{:S(2)}) copy-start(bf16[192,768]{1,0:T(8,128)(2,1)} %param.8) | copy-start | bytes 884740
  15.7 206.1 %all-reduce.8.cloned.1.call-start = ((), (), s32[]{:S(2)}) async-start(), calls=%async_computation.1 | async-start | bytes 393216 | tf_op jit(solution)/shard_map/psum | solution.py:53
  152.1 284.9 %all-reduce.10.cloned.1.call-start = ((), (), s32[]{:S(2)}) async-start(), calls=%async_computation.2 | async-start | bytes 5898240 | tf_op jit(solution)/shard_map/psum | solution.py:50
  221.8 4.9 %copy-start.1 = (bf16[64,32,768]{2,1,0:T(8,128)(2,1)S(1)}, bf16[64,32,768]{2,1,0:T(8,128)(2,1)}, u32[]{:S(2)}) copy-start(bf16[64,32,768]{2,1,0:T(8,128)(2,1)} %param.10) | copy-start | bytes 9437188
  226.7 1.5 copy-start.3
  228.9 16.2 %copy-start.6 = (f32[64,768]{1,0:T(8,128)S(1)}, f32[64,768]{1,0:T(8,128)}, u32[]{:S(2)}) copy-start(f32[64,768]{1,0:T(8,128)} %param.15) | copy-start | bytes 589828
  228.9 16.2 %copy-start.7 = (f32[64,768]{1,0:T(8,128)S(1)}, f32[64,768]{1,0:T(8,128)}, u32[]{:S(2)}) copy-start(f32[64,768]{1,0:T(8,128)} %param.14) | copy-start | bytes 589828
Sparse Core Ops, SparseCore 0:
  15.8 78.1 all-reduce.5
  152.2 69.5 all-reduce.7
  230.6 206.4 all-reduce.9
